TPU v7x, 32 devices: a whole 2x2x4 slice. The times are simulated.
32 devices in a mesh: replica: 8 (over y, x, core), tensor: 4 (over z).
Axes of the slice: x: 2, y: 2, z: 4, core: 2. Of those that a mesh axis runs over, the one named last changes fastest.
Arguments:
- attention_heads_output: bfloat16 [2048, 8192], P('replica', 'tensor'), may hold values from -6 to 6
- output_projection_weight: bfloat16 [8192, 8192], P('tensor'), may hold values from -0.0625 to 0.0625
- adapter_down_factors: bfloat16 [512, 64, 8192], P(None, 'replica', 'tensor'), may hold values from -0.0625 to 0.0625
- adapter_up_factors: bfloat16 [512, 64, 8192], P(None, 'replica', 'tensor'), may hold values from -0.75 to 0.75
- group_working_adapters: int32 [8, 8], replicated, may hold values from 0 to 511, as said below
- adapter_store_row: int32 [512], replicated, may hold values from 0 to 511, each once
- request_working_slot: int32 [2048], P('replica'), may hold values from 0 to 7
Outputs:
- projected: bfloat16 [2048, 8192], P('replica', 'tensor')
Inputs may be any that keep to these rules, and one draw needn't show every extreme that they name: `group_working_adapters`: the 8 ids of one group are distinct. `adapter_store_row`: each adapter has its own row.
All inputs are finite; a program needn't handle non-finite values.
Results may differ from a plain program's by a relative error of at most 0.0028.
Values may be sent and summed in bfloat16 or wider, within the bound.
A program may use at most 128 MiB of HBM per device.

v0:
```python
import jax
import jax.numpy as jnp
from jax import lax
from jax.sharding import PartitionSpec as P

ADAPTER_RANK = 64
WORKING_SLOTS = 8


ADAPTER_SCALE = 0.5


def body(
    attention_heads_output,
    output_projection_weight,
    adapter_down_factors,
    adapter_up_factors,
    group_working_adapters,
    adapter_store_row,
    request_working_slot,
):
    groups = lax.axis_size("replica")
    row_count, features = attention_heads_output.shape
    local_rank_count = adapter_down_factors.shape[1]
    needed_store_rows = jnp.take(adapter_store_row, group_working_adapters.reshape(-1), axis=0)
    outgoing_down_factors = jnp.take(adapter_down_factors, needed_store_rows, axis=0)
    outgoing_up_factors = jnp.take(adapter_up_factors, needed_store_rows, axis=0)
    outgoing = jnp.stack([outgoing_down_factors, outgoing_up_factors], axis=1).reshape(
        groups, WORKING_SLOTS, 2, local_rank_count * features
    )
    fetched = lax.all_to_all(outgoing, "replica", split_axis=0, concat_axis=0, tiled=True)
    fetched = fetched.reshape(groups, WORKING_SLOTS, 2, local_rank_count, features).transpose(
        2, 1, 0, 3, 4
    )
    fetched = fetched.reshape(2, WORKING_SLOTS * ADAPTER_RANK, features)
    down_factor_rows = fetched[0]
    up_factor_rows = fetched[1]
    selector = (
        request_working_slot[:, None] == jnp.arange(WORKING_SLOTS, dtype=jnp.int32)[None, :]
    ).astype(jnp.float32)
    all_ranks = lax.dot_general(
        attention_heads_output,
        down_factor_rows,
        (((1,), (1,)), ((), ())),
        preferred_element_type=jnp.float32,
    )
    rank_local = jnp.sum(
        all_ranks.reshape(row_count, WORKING_SLOTS, ADAPTER_RANK) * selector[:, :, None], axis=1
    )
    base_local = jnp.dot(
        attention_heads_output, output_projection_weight, preferred_element_type=jnp.float32
    )
    base_projection_sum = lax.psum_scatter(base_local, "tensor", scatter_dimension=1, tiled=True)
    rank_total = lax.psum(rank_local, "tensor")
    rounded = rank_total.astype(jnp.bfloat16)
    expanded = (rounded[:, None, :] * selector[:, :, None].astype(jnp.bfloat16)).reshape(
        row_count, WORKING_SLOTS * ADAPTER_RANK
    )
    adapter_contribution = jnp.dot(expanded, up_factor_rows, preferred_element_type=jnp.float32)
    return (base_projection_sum + ADAPTER_SCALE * adapter_contribution).astype(jnp.bfloat16)


def solution(mesh):
    in_specs = (
        P("replica", "tensor"),
        P("tensor", None),
        P(None, "replica", "tensor"),
        P(None, "replica", "tensor"),
        P(),
        P(),
        P("replica"),
    )
    out_specs = P("replica", "tensor")
    return jax.shard_map(body, mesh=mesh, in_specs=in_specs, out_specs=out_specs, check_vma=False)
```

profile of v0, /device:TPU:16, one launch (start us, length us, event | category | flops | bytes accessed | tf_op | source)
XLA Modules:
  0.0 183.5 jit_solution(9984006710890485887)
XLA Ops:
  6.5 0.0 copy-start
  6.5 0.0 reduce-scatter.2.cloned.1.call-start
  6.5 1.2 copy-done
  7.8 17.0 %fusion.6 = f32[256,8192]{1,0:T(8,128)} fusion(bf16[256,2048]{1,0:T(8,128)(2,1)S(1)} %copy-done, bf16[2048,8192]{1,0:T(8,128)(2,1)} %param.10), kind=kOutput, calls=%fused_computation.24 | convolution fusion | flops 8589934592 | bytes 42991616 | tf_op jit(solution)/shard_map/dot_general | solution.py:50
  24.7 0.0 copy-start.3
  24.7 0.0 copy-start.1
  24.7 0.0 reduce-scatter.2.cloned.1.call-update
  24.8 0.7 copy-done.3
  25.4 0.1 reshape.116
  25.5 0.1 reshape.115
  25.6 0.0 copy-done.1
  25.6 0.8 gather_fusion
  26.4 6.5 %gather_fusion.1 = bf16[64,8,2048]{2,1,0:T(8,128)(2,1)S(1)} fusion(bf16[512,8,2048]{2,1,0:T(8,128)(2,1)} %param.11, s32[1024]{0:T(1024)S(1)} %pad_clamp_fusion), kind=kCustom, calls=%fused_computation.clone | custom fusion | bytes 4194560 | tf_op jit(solution)/shard_map/jit(_take)/gather | solution.py:26
  32.9 7.9 %gather_fusion.2 = bf16[64,8,2048]{2,1,0:T(8,128)(2,1)} fusion(bf16[512,8,2048]{2,1,0:T(8,128)(2,1)} %param.12, s32[1024]{0:T(1024)S(1)} %pad_clamp_fusion), kind=kCustom, calls=%fused_computation.1.clone | custom fusion | bytes 4194560 | tf_op jit(solution)/shard_map/jit(_take)/gather | solution.py:27
  40.8 4.2 %broadcast_select_fusion.1 = (bf16[64,8,2048]{2,1,0:T(8,128)(2,1)}, bf16[64,8,2048]{2,1,0:T(8,128)(2,1)}) fusion(bf16[64,8,2048]{2,1,0:T(8,128)(2,1)S(1)} %gather_fusion.1, pred[64]{0:T(512)(128)(4,1)S(1)} %get-tuple-element.6, bf16[64,8,2048]{2,1,0:T(8,128)(2,1)} %gather_fusion.2), kind=kLoop, calls=%fused_computation.9 | loop fusion | flops 2097152 | bytes 8388672 | tf_op jit(solution)/shard_map/jit(_take)/select_n | solution.py:26
  44.9 0.0 copy-start.2
  44.9 4.4 %stack.10 = bf16[8,8,1,16384]{3,1,2,0:T(8,128)(2,1)} reshape(bf16[64,8,2048]{2,1,0:T(8,128)(2,1)} %get-tuple-element.13) | data formatting | bytes 4194304 | tf_op jit(solution)/shard_map/stack | solution.py:28
  49.3 0.0 copy-done.2
  49.3 2.4 %stack.9 = bf16[8,8,1,16384]{3,1,2,0:T(8,128)(2,1)} reshape(bf16[64,8,2048]{2,1,0:T(8,128)(2,1)S(1)} %copy-done.2) | data formatting | bytes 4194304 | tf_op jit(solution)/shard_map/stack | solution.py:28
  51.7 4.7 %pad_maximum_fusion = bf16[8,8,2,16384]{3,1,2,0:T(8,128)(2,1)} fusion(bf16[8,8,1,16384]{3,1,2,0:T(8,128)(2,1)} %stack.10, bf16[8,8,1,16384]{3,1,2,0:T(8,128)(2,1)} %stack.9), kind=kLoop, calls=%fused_computation.3 | loop fusion | flops 2097152 | bytes 8388608 | tf_op jit(solution)/shard_map/stack | solution.py:28
  56.3 0.0 copy-start.4
  56.3 4.7 %all-to-all-start = ((bf16[8,8,2,16384]{3,1,2,0:T(8,128)(2,1)}), bf16[8,8,2,16384]{3,1,2,0:T(8,128)(2,1)}, u32[]{:S(2)}, u32[]{:S(2)}) async-start(bf16[8,8,2,16384]{3,1,2,0:T(8,128)(2,1)} %pad_maximum_fusion), calls=%async_computation.1 | async-start | bytes 8388608 | tf_op jit(solution)/shard_map/all_to_all | solution.py:31
  61.0 0.0 copy-done.4
  61.0 49.1 %all-to-all-done = bf16[8,8,2,16384]{3,1,2,0:T(8,128)(2,1)} async-done(((bf16[8,8,2,16384]{3,1,2,0:T(8,128)(2,1)}), bf16[8,8,2,16384]{3,1,2,0:T(8,128)(2,1)}, u32[]{:S(2)}, u32[]{:S(2)}) %all-to-all-start) | async-done | bytes 4194336 | tf_op jit(solution)/shard_map/all_to_all | solution.py:31
  110.1 5.0 %copy.13 = bf16[16,8,8,2048]{3,2,1,0:T(8,128)(2,1)S(1)} copy(bf16[16,8,8,2048]{3,1,2,0:T(8,128)(2,1)} %bitcast.11) | data formatting | bytes 8388608
  115.1 0.6 copy.15
  115.7 0.4 fusion.5
  116.1 0.7 fusion.7
  116.9 20.5 %psum.7 = bf16[256,64]{0,1:T(8,128)(2,1)S(1)} all-reduce(f32[256,64]{0,1:T(8,128)S(1)} %multiply_reduce_fusion), channel_id=1, replica_groups=mesh['replica'=8,'tensor'=4] {'tensor'}, use_global_device_ids=true, to_apply=%region_2.4 | all-reduce | flops 16384 | bytes 98304 | tf_op jit(solution)/shard_map/psum | solution.py:54
  137.5 35.8 %reduce-scatter.2.cloned.1.call-done = f32[256,2048]{1,0:T(8,128)} async-done(((f32[256,8192]{1,0:T(8,128)}), f32[256,2048]{1,0:T(8,128)}) %reduce-scatter.2.cloned.1.call-update) | async-done | bytes 2097168 | tf_op jit(solution)/shard_map/reduce_scatter | solution.py:53
  173.3 3.3 %fusion.1 = bf16[256,2048]{1,0:T(8,128)(2,1)} fusion(f32[256,2048]{1,0:T(8,128)} %reduce-scatter.2.cloned.1.call-done, bf16[256,512]{0,1:T(8,128)(2,1)S(1)} %bitcast.28, bf16[512,2048]{1,0:T(8,128)(2,1)S(1)} %bitcast.26), kind=kOutput, calls=%fused_computation.7 | convolution fusion | flops 538443776 | bytes 5505024 | tf_op jit(solution)/shard_map/dot_general | solution.py:59
  (7 shorter events, 0.1 us)
Async XLA Ops:
  6.5 1.2 copy-start
  6.5 166.8 %reduce-scatter.2.cloned.1.call-start = ((), (), s32[]{:S(2)}) async-start(), calls=%async_computation.2 | async-start | bytes 10485760 | tf_op jit(solution)/shard_map/reduce_scatter | solution.py:53
  24.7 0.7 copy-start.3
  24.7 0.9 copy-start.1
  44.9 4.4 %copy-start.2 = (bf16[64,8,2048]{2,1,0:T(8,128)(2,1)S(1)}, bf16[64,8,2048]{2,1,0:T(8,128)(2,1)}, u32[]{:S(2)}) copy-start(bf16[64,8,2048]{2,1,0:T(8,128)(2,1)} %get-tuple-element.12) | copy-start | bytes 6291460
  56.3 4.7 %copy-start.4 = (s32[256]{0:T(256)S(1)}, s32[256]{0:T(256)}, u32[]{:S(2)}) copy-start(s32[256]{0:T(256)} %param.15) | copy-start | bytes 3076
  56.3 53.8 %all-to-all-start = ((bf16[8,8,2,16384]{3,1,2,0:T(8,128)(2,1)}), bf16[8,8,2,16384]{3,1,2,0:T(8,128)(2,1)}, u32[]{:S(2)}, u32[]{:S(2)}) async-start(bf16[8,8,2,16384]{3,1,2,0:T(8,128)(2,1)} %pad_maximum_fusion), calls=%async_computation.1 | async-start | bytes 8388608 | tf_op jit(solution)/shard_map/all_to_all | solution.py:31
Sparse Core Ops, SparseCore 0:
  24.9 148.3 reduce-scatter.1
where the time goes:
time: 185 us; the launch traced here: 183 us
  waiting for transfers between devices  84.9 us (46%)
  local copies, waits for them, and re-layouts  29.8 us (16%)
  matrix products  21 us (11%)
  blocking collectives  20.5 us (11%)
  between operations  13.5 us (7%)
  other arithmetic  8.92 us (5%)
  starting transfers between devices  4.71 us (3%)
    all_to_all x1, waiting for transfers between devices, body(): lax.all_to_all(outgoing, 'replica', split_axis=0, concat_axis=0, tiled=True)  49.1 us
    reduce_scatter x1, waiting for transfers between devices, body(): lax.psum_scatter(base_local, 'tensor', scatter_dimension=1, tiled=True)  35.8 us
    psum x1, blocking collectives, body(): rank_total = lax.psum(rank_local, 'tensor')  20.5 us
    dot_general x1, matrix products, body(): jnp.dot(attention_heads_output, output_projection_weight, preferred_eleme...  17 us
    gather x1, local copies, waits for them, and re-layouts, body(): jnp.take(adapter_up_factors, needed_store_rows, axis=0)  7.86 us
    unnamed x11, local copies, waits for them, and re-layouts  6.88 us
    another operation x2, local copies, waits for them, and re-layouts, body(): jnp.stack([outgoing_down_factors, outgoing_up_factors], axis=1)  6.71 us
    gather x1, local copies, waits for them, and re-layouts, body(): jnp.take(adapter_down_factors, needed_store_rows, axis=0)  6.45 us
  transfers between devices with their start and end apart: 2, of which 2 were waited for; matrix products, arithmetic and copies ran while one was open for 21% of the time, Pallas kernels for 0%

commit v1 on v0

--- a/solution.py
+++ b/solution.py
@@ -1,6 +1,10 @@
+import functools
+
 import jax
 import jax.numpy as jnp
 from jax import lax
+from jax.experimental import pallas as pl
+from jax.experimental.pallas import tpu as pltpu
 from jax.sharding import PartitionSpec as P
 
 ADAPTER_RANK = 64
@@ -60,6 +64,325 @@
     return (base_projection_sum + ADAPTER_SCALE * adapter_contribution).astype(jnp.bfloat16)
 
 
+MESH = pl.DeviceIdType.MESH
+ANY = pl.BlockSpec(memory_space=pl.ANY)
+VMEM = pl.BlockSpec(memory_space=pltpu.VMEM)
+SMEM = pl.BlockSpec(memory_space=pltpu.SMEM)
+F32 = jnp.float32
+BF16 = jnp.bfloat16
+
+LINE = 4
+SUB = 4
+BLOCKS = LINE * SUB
+SLOTS_W = 4
+
+
+def gather_kernel(ids, store, down, up, out_down, out_up, sems):
+    count = out_down.shape[0]
+
+    def copies(i, row):
+        return (
+            pltpu.make_async_copy(down.at[row], out_down.at[i], sems.at[0, i]),
+            pltpu.make_async_copy(up.at[row], out_up.at[i], sems.at[1, i]),
+        )
+
+    def start(i, carry):
+        for copy in copies(i, store[ids[i // WORKING_SLOTS, i % WORKING_SLOTS]]):
+            copy.start()
+        return carry
+
+    def finish(i, carry):
+        for copy in copies(i, 0):
+            copy.wait()
+        return carry
+
+    lax.fori_loop(0, count, start, 0)
+    lax.fori_loop(0, count, finish, 0)
+
+
+def fold_matrix(columns, ranks, half):
+    c = lax.broadcasted_iota(jnp.int32, (columns, 2 * ranks), 0)
+    t = lax.broadcasted_iota(jnp.int32, (columns, 2 * ranks), 1)
+    target = (c // (WORKING_SLOTS * 8)) * 8 + c % 8 + half * ranks
+    return jnp.where(target == t, 1.0, 0.0).astype(BF16)
+
+
+def spread_matrix(columns, ranks, half):
+    t = lax.broadcasted_iota(jnp.int32, (2 * ranks, columns), 0)
+    c = lax.broadcasted_iota(jnp.int32, (2 * ranks, columns), 1)
+    target = (c // (WORKING_SLOTS * 8)) * 8 + c % 8 + half * ranks
+    return jnp.where(target == t, 1.0, 0.0).astype(BF16)
+
+
+def main_kernel(
+    groups,
+    x_ref, slot_ref, w_ref, down_ref, up_ref, out_ref,
+    wbuf, acc, sbuf, from_end, from_mid, from_far, got_down, got_up, term,
+    rank_own, rank_end, rank_far, rank_total,
+    w_sem, send_sem, end_sem, mid_sem, far_sem, fetch_send, fetch_recv, own_sem, rank_send, rank_recv,
+):
+    me = lax.axis_index("replica")
+    z = lax.axis_index("tensor")
+    upper = z // 2
+    inner = (z + upper) % 2
+    is_end = inner == 0
+    is_mid = inner == 1
+    beside = 3 * upper + (1 - 2 * upper) * (1 - inner)
+    far_mid = 3 * upper + (1 - 2 * upper) * 2
+    far_end = 3 * upper + (1 - 2 * upper) * 3
+
+    rows, depth = x_ref.shape
+    width = out_ref.shape[1] // SUB
+    ranks = ADAPTER_RANK
+    fetched = groups * WORKING_SLOTS * 8
+
+    def w_copy(p, slot):
+        place = (3 + inner - p // SUB + LINE) % LINE
+        chunk = 3 * upper + (1 - 2 * upper) * place
+        column = pl.multiple_of((chunk * SUB + p % SUB) * width, width)
+        return pltpu.make_async_copy(w_ref.at[:, pl.ds(column, width)], wbuf.at[slot], w_sem.at[slot])
+
+    for p in range(SLOTS_W):
+        w_copy(p, p).start()
+
+    barrier = pltpu.get_barrier_semaphore()
+    for k in range(1, groups):
+        pl.semaphore_signal(barrier, inc=1, device_id=((me + k) % groups, z), device_id_type=MESH)
+    for k in range(1, LINE):
+        pl.semaphore_signal(barrier, inc=1, device_id=(me, (z + k) % LINE), device_id_type=MESH)
+    pl.semaphore_wait(barrier, groups - 1 + LINE - 1)
+
+    def fetch(which, k):
+        src, dst = ((down_ref, got_down), (up_ref, got_up))[which]
+        to = (me + k) % groups
+        return pltpu.make_async_remote_copy(
+            src_ref=src.at[to], dst_ref=dst.at[me],
+            send_sem=fetch_send.at[which, k], recv_sem=fetch_recv.at[which, k],
+            device_id=(to, z), device_id_type=MESH,
+        )
+
+    def fetch_own(which):
+        src, dst = ((down_ref, got_down), (up_ref, got_up))[which]
+        return pltpu.make_async_copy(src.at[me], dst.at[me], own_sem.at[which])
+
+    def fetch_start(which):
+        for k in range(1, groups):
+            fetch(which, k).start()
+        fetch_own(which).start()
+
+    def fetch_wait(which):
+        for k in range(1, groups):
+            fetch(which, k).wait()
+        fetch_own(which).wait()
+
+    def to_beside_mid(p):
+        return pltpu.make_async_remote_copy(
+            src_ref=sbuf.at[p], dst_ref=from_end.at[p], send_sem=send_sem.at[p], recv_sem=end_sem.at[p],
+            device_id=(me, beside), device_id_type=MESH)
+
+    def to_beside_end(p):
+        return pltpu.make_async_remote_copy(
+            src_ref=sbuf.at[p], dst_ref=from_mid.at[p], send_sem=send_sem.at[p], recv_sem=mid_sem.at[p],
+            device_id=(me, beside), device_id_type=MESH)
+
+    def to_far(p, j, device):
+        return pltpu.make_async_remote_copy(
+            src_ref=sbuf.at[p], dst_ref=from_far.at[j], send_sem=send_sem.at[p], recv_sem=far_sem.at[j],
+            device_id=(me, device), device_id_type=MESH)
+
+    fetch_start(0)
+
+    def block(p, carry):
+        slot = p % SLOTS_W
+        w_copy(p, slot).wait()
+        part = jnp.dot(x_ref[...], wbuf[slot], preferred_element_type=F32)
+        sent = jnp.where(is_end, p < 3 * SUB, p < SUB)
+
+        @pl.when(sent)
+        def _():
+            sbuf[p] = part.astype(BF16)
+
+        @pl.when(jnp.logical_not(sent))
+        def _():
+            acc[p - SUB] = part
+
+        @pl.when(jnp.logical_and(is_end, sent))
+        def _():
+            to_beside_mid(p).start()
+
+        @pl.when(jnp.logical_and(is_mid, sent))
+        def _():
+            to_beside_end(p).start()
+
+        @pl.when(p + SLOTS_W < BLOCKS)
+        def _():
+            w_copy(p + SLOTS_W, slot).start()
+
+        return carry
+
+    lax.fori_loop(0, BLOCKS, block, 0)
+    fetch_start(1)
+
+    def merge(p, carry):
+        to_beside_mid(p - SUB).wait_recv()
+        sbuf[p] = (acc[p - SUB] + from_end[p - SUB].astype(F32)).astype(BF16)
+        return carry
+
+    def merge_far_end(j, carry):
+        merge(SUB + j, carry)
+        to_far(SUB + j, j, far_end).start()
+        return carry
+
+    def merge_far_mid(j, carry):
+        merge(2 * SUB + j, carry)
+        to_far(2 * SUB + j, j, far_mid).start()
+        return carry
+
+    fetch_wait(0)
+    down_rows = got_down[...].astype(F32).reshape(fetched, depth).astype(BF16)
+    every = lax.dot_general(x_ref[...], down_rows, (((1,), (1,)), ((), ())), preferred_element_type=F32)
+    column_slot = (lax.broadcasted_iota(jnp.int32, (rows, fetched), 1) // 8) % WORKING_SLOTS
+    chosen = slot_ref[...] == column_slot
+    every = jnp.where(chosen, every, 0.0)
+    half = rows // 2
+    total = jnp.zeros((half, 2 * ranks), F32)
+    for h in range(2):
+        rest = every[h * half:(h + 1) * half]
+        matrix = fold_matrix(fetched, ranks, h)
+        for _ in range(3):
+            piece = rest.astype(BF16)
+            total = total + jnp.dot(piece, matrix, preferred_element_type=F32)
+            rest = rest - piece.astype(F32)
+    rank_own[...] = total
+
+    def rank_copy(i, src, dst, device):
+        return pltpu.make_async_remote_copy(
+            src_ref=src, dst_ref=dst, send_sem=rank_send.at[i], recv_sem=rank_recv.at[i],
+            device_id=(me, device), device_id_type=MESH)
+
+    to_mid = rank_copy(0, rank_own, rank_end, beside)
+    across = rank_copy(1, rank_own, rank_far, far_mid)
+    to_end = rank_copy(2, rank_own, rank_total, beside)
+
+    @pl.when(is_end)
+    def _():
+        to_mid.start()
+
+    @pl.when(is_mid)
+    def _():
+        lax.fori_loop(0, SUB, merge_far_end, 0)
+        to_mid.wait_recv()
+        rank_own[...] += rank_end[...]
+        across.start()
+        across.wait_recv()
+        across.wait_send()
+        rank_own[...] += rank_far[...]
+        to_end.start()
+        rank_total[...] = rank_own[...]
+        lax.fori_loop(0, SUB, merge_far_mid, 0)
+        to_end.wait_send()
+
+    @pl.when(is_end)
+    def _():
+        to_mid.wait_send()
+        to_end.wait_recv()
+
+    fetch_wait(1)
+    rounded = rank_total[...].astype(BF16)
+    parts = [
+        jnp.dot(rounded, spread_matrix(fetched, ranks, h), preferred_element_type=F32) for h in range(2)
+    ]
+    expanded = jnp.where(chosen, jnp.concatenate(parts, axis=0), 0.0).astype(BF16)
+    term[...] = got_up[...].astype(F32).reshape(fetched, out_ref.shape[1]).astype(BF16)
+
+    for j in range(SUB):
+        columns = slice(j * width, (j + 1) * width)
+        adapter = jnp.dot(expanded, term[:, columns], preferred_element_type=F32)
+        acc[2 * SUB + j] += ADAPTER_SCALE * adapter
+
+    for j in range(SUB):
+        columns = slice(j * width, (j + 1) * width)
+        to_far(j, j, far_mid).wait_recv()
+
+        @pl.when(is_end)
+        def _():
+            to_beside_end(j).wait_recv()
+            total = acc[2 * SUB + j] + from_mid[j].astype(F32) + from_far[j].astype(F32)
+            out_ref[:, columns] = total.astype(BF16)
+
+        @pl.when(is_mid)
+        def _():
+            to_beside_mid(2 * SUB + j).wait_recv()
+            total = acc[2 * SUB + j] + from_end[2 * SUB + j].astype(F32) + from_far[j].astype(F32)
+            out_ref[:, columns] = total.astype(BF16)
+
+    def drain(p, carry):
+        to_beside_mid(p).wait_send()
+        return carry
+
+    lax.fori_loop(0, 3 * SUB, drain, 0)
+
+
+def line_body(x, w, down, up, ids, store, slots):
+    groups = lax.axis_size("replica")
+    rows, depth = x.shape
+    out_width = w.shape[1] // LINE
+    width = out_width // SUB
+    local_ranks = down.shape[1]
+    needed = groups * WORKING_SLOTS
+    picked_down, picked_up = pl.pallas_call(
+        gather_kernel,
+        out_shape=[
+            jax.ShapeDtypeStruct((needed, local_ranks, down.shape[2]), BF16),
+            jax.ShapeDtypeStruct((needed, local_ranks, up.shape[2]), BF16),
+        ],
+        in_specs=[SMEM, SMEM, ANY, ANY],
+        out_specs=[ANY, ANY],
+        scratch_shapes=[pltpu.SemaphoreType.DMA((2, needed))],
+        name="gather",
+    )(ids, store, down, up)
+    shape = (groups, WORKING_SLOTS, local_ranks)
+    picked_down = picked_down.reshape(shape + (down.shape[2],))
+    picked_up = picked_up.reshape(shape + (up.shape[2],))
+    dma = pltpu.SemaphoreType.DMA
+    half = (rows // 2, 2 * ADAPTER_RANK)
+    return pl.pallas_call(
+        functools.partial(main_kernel, groups),
+        out_shape=jax.ShapeDtypeStruct((rows, out_width), BF16),
+        in_specs=[VMEM, VMEM, ANY, ANY, ANY],
+        out_specs=VMEM,
+        scratch_shapes=[
+            pltpu.VMEM((SLOTS_W, depth, width), BF16),
+            pltpu.VMEM((3 * SUB, rows, width), F32),
+            pltpu.VMEM((3 * SUB, rows, width), BF16),
+            pltpu.VMEM((3 * SUB, rows, width), BF16),
+            pltpu.VMEM((SUB, rows, width), BF16),
+            pltpu.VMEM((SUB, rows, width), BF16),
+            pltpu.VMEM(picked_down.shape, BF16),
+            pltpu.VMEM(picked_up.shape, BF16),
+            pltpu.VMEM((needed * local_ranks, out_width), BF16),
+            pltpu.VMEM(half, F32),
+            pltpu.VMEM(half, F32),
+            pltpu.VMEM(half, F32),
+            pltpu.VMEM(half, F32),
+            dma((SLOTS_W,)),
+            dma((3 * SUB,)),
+            dma((3 * SUB,)),
+            dma((SUB,)),
+            dma((SUB,)),
+            dma((2, groups)),
+            dma((2, groups)),
+            dma((2,)),
+            dma((3,)),
+            dma((3,)),
+        ],
+        compiler_params=pltpu.CompilerParams(
+            collective_id=0, has_side_effects=True, vmem_limit_bytes=56 * 1024 * 1024
+        ),
+        name="project",
+    )(x, slots.reshape(rows, 1), w, picked_down, picked_up)
+
+
 def solution(mesh):
     in_specs = (
         P("replica", "tensor"),
@@ -71,4 +394,6 @@
         P("replica"),
     )
     out_specs = P("replica", "tensor")
-    return jax.shard_map(body, mesh=mesh, in_specs=in_specs, out_specs=out_specs, check_vma=False)
+    on_line = mesh.shape["tensor"] == LINE and mesh.shape["replica"] * 8 == ADAPTER_RANK
+    chosen = line_body if on_line else body
+    return jax.shard_map(chosen, mesh=mesh, in_specs=in_specs, out_specs=out_specs, check_vma=False)

time: 185 us -> 238 us (1.29)
  Pallas kernels: 0 us -> 234 us
  waiting for transfers between devices: 84.9 us -> 0 us
  local copies, waits for them, and re-layouts: 29.8 us -> 3.78 us
  matrix products: 21 us -> 0 us
  blocking collectives: 20.5 us -> 0 us
  between operations: 13.5 us -> 0.02 us
  other arithmetic: 8.92 us -> 0 us
  starting transfers between devices: 4.71 us -> 0 us
    pallas_call x0 -> x2, Pallas kernels: none -> 234 us  [the longest x1 130 us: line_body(): pl.pallas_call(gather_kernel, out_shape=[jax.ShapeDtypeStruct((needed, lo...]
    all_to_all x1 -> x0, waiting for transfers between devices: 49.1 us -> none  [body(): lax.all_to_all(outgoing, 'replica', split_axis=0, concat_axis=0, tiled=True)]
    reduce_scatter x1 -> x0, waiting for transfers between devices: 35.8 us -> none  [body(): lax.psum_scatter(base_local, 'tensor', scatter_dimension=1, tiled=True)]
    dot_general x3 -> x0, matrix products: 21 us -> none  [the longest x1 17 us: body(): jnp.dot(attention_heads_output, output_projection_weight, preferred_eleme...]
    psum x1 -> x0, blocking collectives: 20.5 us -> none  [body(): rank_total = lax.psum(rank_local, 'tensor')]
    gather x3 -> x0, local copies, waits for them, and re-layouts: 15.1 us -> none  [the longest x1 7.86 us: body(): jnp.take(adapter_up_factors, needed_store_rows, axis=0)]
    another operation x2 -> x0, local copies, waits for them, and re-layouts: 6.71 us -> none  [body(): jnp.stack([outgoing_down_factors, outgoing_up_factors], axis=1)]
    all_to_all x1 -> x0, starting transfers between devices: 4.7 us -> none  [body(): lax.all_to_all(outgoing, 'replica', split_axis=0, concat_axis=0, tiled=True)]
  transfers between devices with their start and end apart: 2 -> 0, of which waited for: 2 -> 0; matrix products, arithmetic and copies ran while one was open for 21% -> 0% of each run, Pallas kernels for 0% -> 0%
where the time goes in v1:
time: 238 us
  Pallas kernels  234 us (98%)
  local copies, waits for them, and re-layouts  3.78 us (2%)
    pallas_call x1, Pallas kernels, line_body(): pl.pallas_call(gather_kernel, out_shape=[jax.ShapeDtypeStruct((needed, lo...  130 us
    pallas_call x1, Pallas kernels, line_body(): pl.pallas_call(functools.partial(main_kernel, groups), out_shape=jax.Shap...  104 us

profile of v1, /device:TPU:16, one launch (start us, length us, event | category | flops | bytes accessed | tf_op | source)
XLA Modules:
  0.0 237.9 jit_solution(4921536589167416355)
XLA Ops:
  0.0 1.5 copy.8.slot_ref
  1.5 130.1 %gather.1 = (bf16[64,8,2048]{2,1,0:T(8,128)(2,1)}, bf16[64,8,2048]{2,1,0:T(8,128)(2,1)}) custom-call(s32[8,8]{1,0:T(8,128)} %ids.1, s32[512]{0:T(512)} %store.1, bf16[512,8,2048]{2,1,0:T(8,128)(2,1)} %down.1, bf16[512,8,2048]{2,1,0:T(8,128)(2,1)} %up.1), custom_call_target="tpu_custom_call" | custom-call | tf_op jit(solution)/shard_map/gather/pallas_call | solution.py:333
  131.6 104.1 %project.1 = bf16[256,2048]{1,0:T(8,128)(2,1)} custom-call(bf16[256,2048]{1,0:T(8,128)(2,1)} %x_ref.1, s32[256,1]{1,0:T(8,128)} %copy.8.slot_ref, bf16[2048,8192]{1,0:T(8,128)(2,1)} %w_ref.1, bf16[8,8,8,2048]{3,2,1,0:T(8,128)(2,1)} %bitcast.3, bf16[8,8,8,2048]{3,2,1,0:T(8,128)(2,1)} %bitcast.4), custom_call_target="tpu_custom_call" | custom-call | tf_op jit(solution)/shard_map/project/pallas_call | solution.py:349
  235.6 2.3 copy.10

commit v2 on v1

--- a/solution.py
+++ b/solution.py
@@ -74,30 +74,46 @@
 LINE = 4
 SUB = 4
 BLOCKS = LINE * SUB
+WINDOW = 3
 SLOTS_W = 4
 
 
-def gather_kernel(ids, store, down, up, out_down, out_up, sems):
-    count = out_down.shape[0]
-
-    def copies(i, row):
-        return (
-            pltpu.make_async_copy(down.at[row], out_down.at[i], sems.at[0, i]),
-            pltpu.make_async_copy(up.at[row], out_up.at[i], sems.at[1, i]),
+def gather_kernel(ids, store, down, up, out_down, out_up, got, in_sems, out_sems):
+    groups = out_down.shape[0]
+    pairs = ((down, out_down), (up, out_up))
+
+    def fetch(which, g, j, row):
+        return pltpu.make_async_copy(
+            pairs[which][0].at[row], got.at[which, g, j], in_sems.at[which, g * WORKING_SLOTS + j]
         )
 
-    def start(i, carry):
-        for copy in copies(i, store[ids[i // WORKING_SLOTS, i % WORKING_SLOTS]]):
-            copy.start()
-        return carry
-
-    def finish(i, carry):
-        for copy in copies(i, 0):
-            copy.wait()
-        return carry
-
-    lax.fori_loop(0, count, start, 0)
-    lax.fori_loop(0, count, finish, 0)
+    def put(which, g):
+        return pltpu.make_async_copy(got.at[which, g], pairs[which][1].at[g], out_sems.at[which, g])
+
+    for which in range(2):
+
+        def start(g, carry):
+            for j in range(WORKING_SLOTS):
+                fetch(which, g, j, store[ids[g, j]]).start()
+            return carry
+
+        lax.fori_loop(0, groups, start, 0)
+    for which in range(2):
+
+        def forward(g, carry):
+            for j in range(WORKING_SLOTS):
+                fetch(which, g, j, 0).wait()
+            put(which, g).start()
+            return carry
+
+        lax.fori_loop(0, groups, forward, 0)
+    for which in range(2):
+
+        def finish(g, carry):
+            put(which, g).wait()
+            return carry
+
+        lax.fori_loop(0, groups, finish, 0)
 
 
 def fold_matrix(columns, ranks, half):
@@ -206,7 +222,7 @@
         def _():
             acc[p - SUB] = part
 
-        @pl.when(jnp.logical_and(is_end, sent))
+        @pl.when(jnp.logical_and(is_end, p < WINDOW))
         def _():
             to_beside_mid(p).start()
 
@@ -221,7 +237,11 @@
         return carry
 
     lax.fori_loop(0, BLOCKS, block, 0)
-    fetch_start(1)
+
+    def refill(p, carry):
+        to_beside_mid(p - WINDOW).wait_send()
+        to_beside_mid(p).start()
+        return carry
 
     def merge(p, carry):
         to_beside_mid(p - SUB).wait_recv()
@@ -238,11 +258,23 @@
         to_far(2 * SUB + j, j, far_mid).start()
         return carry
 
+    @pl.when(is_end)
+    def _():
+        lax.fori_loop(WINDOW, 2 * WINDOW, refill, 0)
+
+    @pl.when(is_mid)
+    def _():
+        lax.fori_loop(0, SUB, merge_far_end, 0)
+
     fetch_wait(0)
+    fetch_start(1)
     down_rows = got_down[...].astype(F32).reshape(fetched, depth).astype(BF16)
     every = lax.dot_general(x_ref[...], down_rows, (((1,), (1,)), ((), ())), preferred_element_type=F32)
     column_slot = (lax.broadcasted_iota(jnp.int32, (rows, fetched), 1) // 8) % WORKING_SLOTS
-    chosen = slot_ref[...] == column_slot
+    square = (rows, rows)
+    diagonal = lax.broadcasted_iota(jnp.int32, square, 0) == lax.broadcasted_iota(jnp.int32, square, 1)
+    slot = jnp.sum(jnp.where(diagonal, slot_ref[...].astype(F32), 0.0), axis=1, keepdims=True)
+    chosen = slot == column_slot.astype(F32)
     every = jnp.where(chosen, every, 0.0)
     half = rows // 2
     total = jnp.zeros((half, 2 * ranks), F32)
@@ -267,10 +299,10 @@
     @pl.when(is_end)
     def _():
         to_mid.start()
+        lax.fori_loop(2 * WINDOW, 3 * SUB, refill, 0)
 
     @pl.when(is_mid)
     def _():
-        lax.fori_loop(0, SUB, merge_far_end, 0)
         to_mid.wait_recv()
         rank_own[...] += rank_end[...]
         across.start()
@@ -320,7 +352,11 @@
         to_beside_mid(p).wait_send()
         return carry
 
-    lax.fori_loop(0, 3 * SUB, drain, 0)
+    @pl.when(is_mid)
+    def _():
+        lax.fori_loop(0, 3 * SUB - WINDOW, drain, 0)
+
+    lax.fori_loop(3 * SUB - WINDOW, 3 * SUB, drain, 0)
 
 
 def line_body(x, w, down, up, ids, store, slots):
@@ -330,20 +366,23 @@
     width = out_width // SUB
     local_ranks = down.shape[1]
     needed = groups * WORKING_SLOTS
+    shape = (groups, WORKING_SLOTS, local_ranks)
     picked_down, picked_up = pl.pallas_call(
         gather_kernel,
         out_shape=[
-            jax.ShapeDtypeStruct((needed, local_ranks, down.shape[2]), BF16),
-            jax.ShapeDtypeStruct((needed, local_ranks, up.shape[2]), BF16),
+            jax.ShapeDtypeStruct(shape + (down.shape[2],), BF16),
+            jax.ShapeDtypeStruct(shape + (up.shape[2],), BF16),
         ],
         in_specs=[SMEM, SMEM, ANY, ANY],
         out_specs=[ANY, ANY],
-        scratch_shapes=[pltpu.SemaphoreType.DMA((2, needed))],
+        scratch_shapes=[
+            pltpu.VMEM((2,) + shape + (depth,), BF16),
+            pltpu.SemaphoreType.DMA((2, needed)),
+            pltpu.SemaphoreType.DMA((2, groups)),
+        ],
+        compiler_params=pltpu.CompilerParams(vmem_limit_bytes=56 * 1024 * 1024),
         name="gather",
     )(ids, store, down, up)
-    shape = (groups, WORKING_SLOTS, local_ranks)
-    picked_down = picked_down.reshape(shape + (down.shape[2],))
-    picked_up = picked_up.reshape(shape + (up.shape[2],))
     dma = pltpu.SemaphoreType.DMA
     half = (rows // 2, 2 * ADAPTER_RANK)
     return pl.pallas_call(
@@ -380,7 +419,7 @@
             collective_id=0, has_side_effects=True, vmem_limit_bytes=56 * 1024 * 1024
         ),
         name="project",
-    )(x, slots.reshape(rows, 1), w, picked_down, picked_up)
+    )(x, slots.reshape(1, rows), w, picked_down, picked_up)
 
 
 def solution(mesh):

time: 238 us -> 86.1 us (0.36)
  Pallas kernels: 234 us -> 83.6 us
    pallas_call x1, Pallas kernels: 130 us -> 5.99 us  [line_body(): pl.pallas_call(gather_kernel, out_shape=[jax.ShapeDtypeStruct(shape + (do...]
    pallas_call x1, Pallas kernels: 104 us -> 77.6 us  [line_body(): pl.pallas_call(functools.partial(main_kernel, groups), out_shape=jax.Shap...]
where the time goes in v2:
time: 86.1 us; the launch traced here: 85.9 us
  Pallas kernels  83.6 us (97%)
  local copies, waits for them, and re-layouts  2.3 us (3%)
    pallas_call x1, Pallas kernels, line_body(): pl.pallas_call(functools.partial(main_kernel, groups), out_shape=jax.Shap...  77.6 us
    pallas_call x1, Pallas kernels, line_body(): pl.pallas_call(gather_kernel, out_shape=[jax.ShapeDtypeStruct(shape + (do...  5.99 us
    unnamed x1, local copies, waits for them, and re-layouts  2.3 us

profile of v2, /device:TPU:16, one launch (start us, length us, event | category | flops | bytes accessed | tf_op | source)
XLA Modules:
  0.0 85.9 jit_solution(2058078055456642483)
XLA Ops:
  0.0 6.0 %gather.1 = (bf16[8,8,8,2048]{3,2,1,0:T(8,128)(2,1)}, bf16[8,8,8,2048]{3,2,1,0:T(8,128)(2,1)}) custom-call(s32[8,8]{1,0:T(8,128)} %ids.1, s32[512]{0:T(512)} %store.1, bf16[512,8,2048]{2,1,0:T(8,128)(2,1)} %down.1, bf16[512,8,2048]{2,1,0:T(8,128)(2,1)} %up.1), custom_call_target="tpu_custom_call" | custom-call | tf_op jit(solution)/shard_map/gather/pallas_call | solution.py:370
  6.0 77.6 %project.1 = bf16[256,2048]{1,0:T(8,128)(2,1)} custom-call(bf16[256,2048]{1,0:T(8,128)(2,1)} %x_ref.1, s32[1,256]{1,0:T(1,128)} %bitcast.1, bf16[2048,8192]{1,0:T(8,128)(2,1)} %w_ref.1, bf16[8,8,8,2048]{3,2,1,0:T(8,128)(2,1)} %get-tuple-element.7.down_ref, bf16[8,8,8,2048]{3,2,1,0:T(8,128)(2,1)} %get-tuple-element.8.up_ref), custom_call_target="tpu_custom_call" | custom-call | tf_op jit(solution)/shard_map/project/pallas_call | solution.py:388
  83.6 2.3 %copy.9 = bf16[256,2048]{1,0:T(8,128)(2,1)} copy(bf16[256,2048]{1,0:T(8,128)(2,1)} %project.1) | data formatting | bytes 2097152

commit v3 on v2

--- a/solution.py
+++ b/solution.py
@@ -75,6 +75,7 @@
 SUB = 4
 BLOCKS = LINE * SUB
 WINDOW = 3
+EARLY = 7
 SLOTS_W = 4
 
 
@@ -260,7 +261,7 @@
 
     @pl.when(is_end)
     def _():
-        lax.fori_loop(WINDOW, 2 * WINDOW, refill, 0)
+        lax.fori_loop(WINDOW, EARLY, refill, 0)
 
     @pl.when(is_mid)
     def _():
@@ -299,33 +300,36 @@
     @pl.when(is_end)
     def _():
         to_mid.start()
-        lax.fori_loop(2 * WINDOW, 3 * SUB, refill, 0)
+        lax.fori_loop(EARLY, 3 * SUB, refill, 0)
 
     @pl.when(is_mid)
     def _():
+        lax.fori_loop(0, SUB, merge_far_mid, 0)
         to_mid.wait_recv()
         rank_own[...] += rank_end[...]
         across.start()
+
+    fetch_wait(1)
+    term[...] = got_up[...].astype(F32).reshape(fetched, out_ref.shape[1]).astype(BF16)
+
+    @pl.when(is_mid)
+    def _():
         across.wait_recv()
         across.wait_send()
         rank_own[...] += rank_far[...]
         to_end.start()
         rank_total[...] = rank_own[...]
-        lax.fori_loop(0, SUB, merge_far_mid, 0)
-        to_end.wait_send()
 
     @pl.when(is_end)
     def _():
         to_mid.wait_send()
         to_end.wait_recv()
 
-    fetch_wait(1)
     rounded = rank_total[...].astype(BF16)
     parts = [
         jnp.dot(rounded, spread_matrix(fetched, ranks, h), preferred_element_type=F32) for h in range(2)
     ]
     expanded = jnp.where(chosen, jnp.concatenate(parts, axis=0), 0.0).astype(BF16)
-    term[...] = got_up[...].astype(F32).reshape(fetched, out_ref.shape[1]).astype(BF16)
 
     for j in range(SUB):
         columns = slice(j * width, (j + 1) * width)
@@ -354,6 +358,7 @@
 
     @pl.when(is_mid)
     def _():
+        to_end.wait_send()
         lax.fori_loop(0, 3 * SUB - WINDOW, drain, 0)
 
     lax.fori_loop(3 * SUB - WINDOW, 3 * SUB, drain, 0)

time: 86.1 us -> 86.1 us (level)
  no operation moved by 1% of the time
where the time goes in v3:
time: 86.1 us; the launch traced here: 85.8 us
  Pallas kernels  83.5 us (97%)
  local copies, waits for them, and re-layouts  2.3 us (3%)
    pallas_call x1, Pallas kernels, line_body(): pl.pallas_call(functools.partial(main_kernel, groups), out_shape=jax.Shap...  77.6 us
    pallas_call x1, Pallas kernels, line_body(): pl.pallas_call(gather_kernel, out_shape=[jax.ShapeDtypeStruct(shape + (do...  5.89 us
    unnamed x1, local copies, waits for them, and re-layouts  2.3 us

profile of v3, /device:TPU:16, one launch (start us, length us, event | category | flops | bytes accessed | tf_op | source)
XLA Modules:
  0.0 85.8 jit_solution(13619712856165426975)
XLA Ops:
  0.0 5.9 %gather.1 = (bf16[8,8,8,2048]{3,2,1,0:T(8,128)(2,1)}, bf16[8,8,8,2048]{3,2,1,0:T(8,128)(2,1)}) custom-call(s32[8,8]{1,0:T(8,128)} %ids.1, s32[512]{0:T(512)} %store.1, bf16[512,8,2048]{2,1,0:T(8,128)(2,1)} %down.1, bf16[512,8,2048]{2,1,0:T(8,128)(2,1)} %up.1), custom_call_target="tpu_custom_call" | custom-call | tf_op jit(solution)/shard_map/gather/pallas_call | solution.py:375
  5.9 77.6 %project.1 = bf16[256,2048]{1,0:T(8,128)(2,1)} custom-call(bf16[256,2048]{1,0:T(8,128)(2,1)} %x_ref.1, s32[1,256]{1,0:T(1,128)} %bitcast.1, bf16[2048,8192]{1,0:T(8,128)(2,1)} %w_ref.1, bf16[8,8,8,2048]{3,2,1,0:T(8,128)(2,1)} %get-tuple-element.7.down_ref, bf16[8,8,8,2048]{3,2,1,0:T(8,128)(2,1)} %get-tuple-element.8.up_ref), custom_call_target="tpu_custom_call" | custom-call | tf_op jit(solution)/shard_map/project/pallas_call | solution.py:393
  83.5 2.3 %copy.9 = bf16[256,2048]{1,0:T(8,128)(2,1)} copy(bf16[256,2048]{1,0:T(8,128)(2,1)} %project.1) | data formatting | bytes 2097152
